TPU v7x, 32 devices: a whole 2x2x4 slice. The times are simulated.
32 devices in a mesh: lon: 16 (over z, y, core), lat: 2 (over x).
Axes of the slice: x: 2, y: 2, z: 4, core: 2. Of those that a mesh axis runs over, the one named last changes fastest.
Arguments:
- fine_tokens: bfloat16 [72, 384, 512], P('lat', 'lon'), may hold values from -6 to 6
- fine_qkv: bfloat16 [512, 1536], replicated, may hold values from -0.25 to 0.25
- fine_scale: float32 [8], replicated, may hold values from 3 to 15
- fine_proj: bfloat16 [512, 512], replicated, may hold values from -0.25 to 0.25
- window_mask: int32 [13, 32], replicated, may hold values from 0 to 3
- merge_weight: bfloat16 [2048, 1024], replicated, may hold values from -0.125 to 0.125
- mid_qkv: bfloat16 [1024, 1536], replicated, may hold values from -0.1875 to 0.1875
- mid_scale: float32 [8], replicated, may hold values from 3 to 15
- mid_proj: bfloat16 [512, 1024], replicated, may hold values from -0.25 to 0.25
Outputs:
- fine_out: bfloat16 [72, 384, 512], P('lat', 'lon')
- mid_out: bfloat16 [36, 192, 1024], P('lat', 'lon')
Inputs may be any that keep to these rules, and one draw needn't show every extreme that they name: `window_mask`: the bit of value 1 in a window's mask splits its upper and lower halves, the bit of value 2 its western and eastern halves.
All inputs are finite; a program needn't handle non-finite values.
Results may differ from a plain program's by a relative error of at most 0.015.
Values may be sent and summed in bfloat16 or wider, within the bound.
A program may use at most 128 MiB of HBM per device.

v0:
```python
import jax
import jax.numpy as jnp
from jax import lax
from jax.sharding import PartitionSpec as P

WLAT = 6
WLON = 12


EPS_NORM = 1e-05
EPS_DIR = 1e-06


def extended(cells, sides, width, closed):
    for axis, dim in sides:
        count = lax.axis_size(axis)
        ends = count if closed else count - 1
        head = lax.slice_in_dim(cells, 0, width, axis=dim)
        tail = lax.slice_in_dim(cells, cells.shape[dim] - width, cells.shape[dim], axis=dim)
        cells = jnp.concatenate(
            [
                lax.ppermute(tail, axis, [(i, (i + 1) % count) for i in range(ends)]),
                cells,
                lax.ppermute(head, axis, [((i + 1) % count, i) for i in range(ends)]),
            ],
            axis=dim,
        )
    return cells


def layer_norm(values):
    mean = jnp.mean(values, axis=-1, keepdims=True)
    centred = values - mean
    var = jnp.mean(centred * centred, axis=-1, keepdims=True)
    return centred * lax.rsqrt(var + EPS_NORM)


def attend(query, keys, values, scale, allowed):
    raw = jnp.einsum("wqhe,wkhe->whqk", query, keys, preferred_element_type=jnp.float32)
    query_sq = jnp.einsum("wqhe,wqhe->whq", query, query, preferred_element_type=jnp.float32)
    keys_sq = jnp.einsum("wkhe,wkhe->whk", keys, keys, preferred_element_type=jnp.float32)
    cosine = (
        raw
        * lax.rsqrt(query_sq + EPS_DIR)[:, :, :, None]
        * lax.rsqrt(keys_sq + EPS_DIR)[:, :, None, :]
    )
    expo = jnp.where(
        allowed[:, None], jnp.exp(scale[None, :, None, None] * cosine), jnp.float32(0.0)
    )
    weights = (expo / jnp.sum(expo, axis=-1, keepdims=True)).astype(jnp.bfloat16)
    mixed = jnp.einsum("whqk,wkhe->wqhe", weights, values, preferred_element_type=jnp.float32)
    return mixed.astype(jnp.bfloat16)


def per_device(
    fine_tokens,
    fine_qkv,
    fine_scale,
    fine_proj,
    window_mask,
    merge_weight,
    mid_qkv,
    mid_scale,
    mid_proj,
):
    rows, cols, width = fine_tokens.shape
    heads = fine_scale.shape[0]
    head_dim = width // heads
    half_lat = WLAT // 2
    half_lon = WLON // 2
    place = WLAT * WLON
    lat_index = lax.axis_index("lat")
    lon_index = lax.axis_index("lon")
    lat_total = rows * lax.axis_size("lat")
    projected_all = jnp.dot(fine_tokens, fine_qkv, preferred_element_type=jnp.float32).astype(
        jnp.bfloat16
    )
    query = projected_all[..., :width]
    shipped = projected_all[..., width:]
    beside_all = extended(shipped, (("lon", 1),), half_lon, True)
    border = extended(beside_all, (("lat", 0),), half_lat, False)
    ext_rows = rows + WLAT
    ext_cols = cols + WLON
    band_count = ext_rows // WLAT
    col_count = ext_cols // WLON
    win_count = band_count * col_count

    def to_windows(grid):
        return (
            grid.reshape(band_count, WLAT, col_count, WLON, grid.shape[-1])
            .transpose(0, 2, 1, 3, 4)
            .reshape(win_count, place, grid.shape[-1])
        )

    padded_query = jnp.pad(query, ((half_lat, half_lat), (half_lon, half_lon), (0, 0)))
    win_query = to_windows(padded_query).reshape(win_count, place, heads, head_dim)
    win_kv = to_windows(border).reshape(win_count, place, 2, heads, head_dim)
    table = jnp.concatenate([window_mask[:, -1:], window_mask], axis=1)
    row_start = lat_index * (rows // WLAT)
    col_start = lon_index * (cols // WLON)
    local_pattern = lax.dynamic_slice(
        table, (row_start, col_start), (band_count, col_count)
    ).reshape(-1)
    glob_row = lat_index * rows - half_lat + jnp.arange(ext_rows, dtype=jnp.int32)
    valid_rows = ((glob_row >= 0) & (glob_row < lat_total)).reshape(band_count, WLAT)
    valid_key = jnp.broadcast_to(
        valid_rows[:, None, :, None], (band_count, col_count, WLAT, WLON)
    ).reshape(win_count, place)
    lat_part = jnp.broadcast_to(jnp.arange(WLAT)[:, None] >= half_lat, (WLAT, WLON)).reshape(-1)
    lon_part = jnp.broadcast_to(jnp.arange(WLON)[None, :] >= half_lon, (WLAT, WLON)).reshape(-1)
    same_lat = lat_part[:, None] == lat_part[None, :]
    same_lon = lon_part[:, None] == lon_part[None, :]
    split_lat = local_pattern % 2 == 1
    split_lon = local_pattern // 2 == 1
    allowed = (
        valid_key[:, None, :]
        & (jnp.logical_not(split_lat)[:, None, None] | same_lat[None])
        & (jnp.logical_not(split_lon)[:, None, None] | same_lon[None])
    )
    mixed = attend(win_query, win_kv[:, :, 0], win_kv[:, :, 1], fine_scale, allowed)
    mixed = (
        mixed.reshape(band_count, col_count, WLAT, WLON, width)
        .transpose(0, 2, 1, 3, 4)
        .reshape(ext_rows, ext_cols, width)
    )
    own_mixed = mixed[half_lat : half_lat + rows, half_lon : half_lon + cols]
    fine_projected = jnp.dot(own_mixed, fine_proj, preferred_element_type=jnp.float32)
    fine_out = (fine_tokens.astype(jnp.float32) + layer_norm(fine_projected)).astype(jnp.bfloat16)
    coarse_rows = rows // 2
    coarse_cols = cols // 2
    quads = (
        fine_out.reshape(coarse_rows, 2, coarse_cols, 2, width)
        .transpose(0, 2, 3, 1, 4)
        .reshape(coarse_rows, coarse_cols, 4 * width)
    )
    merge_in = layer_norm(quads.astype(jnp.float32)).astype(jnp.bfloat16)
    merged = jnp.dot(merge_in, merge_weight, preferred_element_type=jnp.float32).astype(
        jnp.bfloat16
    )
    mid_heads = mid_scale.shape[0]
    mid_width = mid_heads * head_dim
    mid_act = jnp.dot(merged, mid_qkv, preferred_element_type=jnp.float32).astype(jnp.bfloat16)
    mid_windows = coarse_rows // WLAT
    mid_win_query = mid_act[..., :mid_width].reshape(mid_windows, place, mid_heads, head_dim)
    mid_kv = mid_act[..., mid_width:].reshape(mid_windows, place, 2, mid_heads, head_dim)
    every = jnp.ones((1, 1, 1), dtype=bool)
    mid_mixed = attend(mid_win_query, mid_kv[:, :, 0], mid_kv[:, :, 1], mid_scale, every)
    mid_mixed = mid_mixed.reshape(coarse_rows, coarse_cols, mid_width)
    mid_projected = jnp.dot(mid_mixed, mid_proj, preferred_element_type=jnp.float32)
    mid_out = (merged.astype(jnp.float32) + layer_norm(mid_projected)).astype(jnp.bfloat16)
    return (fine_out, mid_out)


def solution(mesh):
    return jax.shard_map(
        per_device,
        mesh=mesh,
        in_specs=(P("lat", "lon", None), P(), P(), P(), P(), P(), P(), P(), P()),
        out_specs=(P("lat", "lon", None), P("lat", "lon", None)),
        check_vma=False,
    )
```

profile of v0, /device:TPU:0, one launch (start us, length us, event | category | flops | bytes accessed | tf_op | source)
XLA Modules:
  0.0 175.4 jit_solution(17476236269038650277)
XLA Ops:
  0.6 3.4 %convolution_convert_fusion = bf16[36,24,1536]{2,1,0:T(8,128)(2,1)S(1)} fusion(bf16[36,24,512]{2,1,0:T(8,128)(2,1)} %param.9, bf16[512,1536]{1,0:T(8,128)(2,1)} %param.10), kind=kOutput, calls=%fused_computation.9 | convolution fusion | flops 1360281600 | bytes 5111808 | tf_op jit(solution)/shard_map/dot_general | solution.py:75
  8.3 5.0 %collective-permute-start.1 = (bf16[36,6,1024]{2,0,1:T(8,128)(2,1)}, bf16[36,6,1024]{2,0,1:T(8,128)(2,1)}, u32[]{:S(2)}, u32[]{:S(2)}) collective-permute-start(bf16[36,6,1024]{2,0,1:T(8,128)(2,1)} %copy.34), channel_id=1, source_target_pairs={{2,0},{4,2},{6,4},{8,6},{10,8},{12,10},{14,12},{16,14},{18,16},{20... | collective-permute-start | bytes 1327112 | tf_op jit(solution)/shard_map/ppermute | solution.py:24
  19.0 2.9 %pad.4 = bf16[42,36,512]{2,1,0:T(8,128)(2,1)} pad(bf16[36,24,512]{2,1,0:T(8,128)(2,1)} %slice.62, bf16[]{:T(256)} %constant.73.clone.1), padding=3_3x6_6x0_0 | pad | bytes 2433026 | tf_op jit(solution)/shard_map/jit(_pad)/pad | solution.py:95
  21.9 3.7 %reshape.227 = bf16[7,6,3,12,512]{4,3,2,1,0:T(8,128)(2,1)} reshape(bf16[42,36,512]{2,1,0:T(8,128)(2,1)} %pad.4) | data formatting | bytes 3096576 | tf_op jit(solution)/shard_map/reshape | solution.py:90
  25.6 3.1 %copy.39 = bf16[7,3,6,12,512]{4,3,2,1,0:T(8,128)(2,1)} copy(bf16[7,3,6,12,512]{4,3,1,2,0:T(8,128)(2,1)} %bitcast.78) | data formatting | bytes 3096576 | tf_op jit(solution)/shard_map/transpose | solution.py:91
  28.7 5.5 %reshape_reshape.7 = bf16[21,72,8,64]{3,2,1,0:T(8,128)(2,1)} reshape(bf16[7,3,6,12,512]{4,3,2,1,0:T(8,128)(2,1)} %copy.39) | data formatting | bytes 3096576 | tf_op jit(solution)/shard_map/reshape;reshape | solution.py:96
  34.2 4.5 %fusion = f32[21,8,72]{1,2,0:T(8,128)} fusion(bf16[21,72,8,64]{3,2,1,0:T(8,128)(2,1)} %reshape_reshape.7), kind=kLoop, calls=%fused_computation.1 | loop fusion | flops 2310336 | bytes 1596672
  43.0 3.9 %collective-permute-start.2 = (bf16[3,36,1024]{2,1,0:T(8,128)(2,1)S(1)}, bf16[3,36,1024]{2,1,0:T(8,128)(2,1)S(1)}, u32[]{:S(2)}, u32[]{:S(2)}) collective-permute-start(bf16[3,36,1024]{2,1,0:T(8,128)(2,1)S(1)} %get-tuple-element.4), channel_id=1, source_target_pairs={{0,1},{2,3},{4,5},{6,7},{8,9},{10,11},{12,13},{14,15},{16,17},{18,... | collective-permute-start | bytes 663560 | tf_op jit(solution)/shard_map/ppermute | solution.py:22
  50.6 4.4 %collective-permute-done.3 = bf16[3,36,1024]{2,1,0:T(8,128)(2,1)S(1)} collective-permute-done((bf16[3,36,1024]{2,1,0:T(8,128)(2,1)S(1)}, bf16[3,36,1024]{2,1,0:T(8,128)(2,1)S(1)}, u32[]{:S(2)}, u32[]{:S(2)}) %collective-permute-start.3) | collective-permute-done | bytes 221216 | tf_op jit(solution)/shard_map/ppermute | solution.py:24
  57.9 6.1 %reshape.225 = bf16[7,6,3,12,1024]{4,3,2,1,0:T(8,128)(2,1)} reshape(bf16[42,36,1024]{2,1,0:T(8,128)(2,1)} %pad_maximum_fusion) | data formatting | bytes 6193152 | tf_op jit(solution)/shard_map/reshape | solution.py:90
  64.0 5.0 %copy.37 = bf16[7,3,6,12,1024]{4,3,2,1,0:T(8,128)(2,1)} copy(bf16[7,3,6,12,1024]{4,3,1,2,0:T(8,128)(2,1)} %bitcast.76) | data formatting | bytes 6193152 | tf_op jit(solution)/shard_map/transpose | solution.py:91
  69.0 9.7 %reshape_reshape.6 = bf16[21,72,2,8,64]{4,3,2,1,0:T(8,128)(2,1)} reshape(bf16[7,3,6,12,1024]{4,3,2,1,0:T(8,128)(2,1)} %copy.37) | data formatting | bytes 6193152 | tf_op jit(solution)/shard_map/reshape;reshape | solution.py:97
  78.7 5.8 %fusion.51 = (bf16[21,72,1,8,64]{4,3,2,1,0:T(8,128)(2,1)}, bf16[21,72,1,8,64]{4,3,2,1,0:T(8,128)(2,1)}) fusion(bf16[21,72,2,8,64]{4,3,2,1,0:T(8,128)(2,1)} %reshape_reshape.6), kind=kLoop, calls=%fused_computation.87 | loop fusion | bytes 6193152 | tf_op jit(solution)/shard_map/slice | solution.py:120
  84.5 5.4 %copy.80 = bf16[21,72,1,8,64]{1,4,3,0,2:T(8,128)(2,1)} copy(bf16[21,72,1,8,64]{4,3,2,1,0:T(8,128)(2,1)} %get-tuple-element.3) | data formatting | bytes 3096576
  92.8 5.4 %copy.79 = bf16[21,72,1,8,64]{1,4,3,0,2:T(8,128)(2,1)} copy(bf16[21,72,1,8,64]{4,3,2,1,0:T(8,128)(2,1)} %get-tuple-element.2) | data formatting | bytes 3096576
  98.3 5.4 %fusion.2 = (f32[21,8,72]{2,1,0:T(8,128)S(1)}, f32[21,8,72,72]{2,3,1,0:T(8,128)S(1)}) fusion(f32[21,8,72]{2,1,0:T(8,128)S(1)} %get-tuple-element.20, f32[21,8,72]{2,1,0:T(8,128)S(1)} %get-tuple-element.21, f32[8]{0:T(128)S(1)} %copy-done.10, pred[21,72,72]{1,2,0:T(8,128)(4,1)S(1)} %or_and_fusion, bf16[21,72,1,8,64]{1,4,3,0,2:T(8,128)(2,1)} %copy.80, ...), kind=kOutput, calls=%fused_computation.6 | convolution fusion | flops 115819200 | bytes 6834272 | tf_op jit(solution)/shard_map/wqhe,wkhe->whqk/dot_general | solution.py:39
  103.7 4.8 %convert_bitcast_fusion = bf16[21,72,8,64]{1,3,2,0:T(8,128)(2,1)} fusion(f32[21,8,72,72]{2,3,1,0:T(8,128)S(1)} %get-tuple-element.13, f32[21,8,72]{2,1,0:T(8,128)S(1)} %get-tuple-element.12, f32[21,8,72]{2,1,0:T(8,128)S(1)} %get-tuple-element.20, f32[21,8,72]{2,1,0:T(8,128)S(1)} %get-tuple-element.21, f32[8]{0:T(128)S(1)} %copy-done.10, ...), kind=kOutput, calls=%fused_computation.19 | convolution fusion | flops 117476352 | bytes 6834272 | tf_op jit(solution)/shard_map/whqk,wkhe->wqhe/dot_general | solution.py:51
  108.6 5.4 %copy.43 = bf16[21,72,8,64]{3,2,1,0:T(8,128)(2,1)} copy(bf16[21,72,8,64]{1,3,2,0:T(8,128)(2,1)} %convert_bitcast_fusion) | data formatting | bytes 3096576 | tf_op jit(solution)/shard_map/convert_element_type | solution.py:52
  114.0 5.6 %reshape.228 = bf16[7,3,6,12,512]{4,3,2,1,0:T(8,128)(2,1)} reshape(bf16[21,72,8,64]{3,2,1,0:T(8,128)(2,1)} %copy.43) | data formatting | bytes 3096576 | tf_op jit(solution)/shard_map/reshape | solution.py:122
  119.6 3.1 %copy.44 = bf16[7,6,3,12,512]{4,3,2,1,0:T(8,128)(2,1)} copy(bf16[7,6,3,12,512]{4,3,1,2,0:T(8,128)(2,1)} %bitcast.77) | data formatting | bytes 3096576 | tf_op jit(solution)/shard_map/transpose | solution.py:123
  122.7 3.7 %reshape.229 = bf16[42,36,512]{2,1,0:T(8,128)(2,1)} reshape(bf16[7,6,3,12,512]{4,3,2,1,0:T(8,128)(2,1)} %copy.44) | data formatting | bytes 3096576 | tf_op jit(solution)/shard_map/reshape | solution.py:124
  130.3 3.2 %reshape.235 = f32[18,2,12,2,512]{4,3,2,1,0:T(2,128)} reshape(bf16[36,24,512]{2,1,0:T(8,128)(2,1)} %add_convert_fusion) | data formatting | bytes 2654208 | tf_op jit(solution)/shard_map/convert_element_type | solution.py:136
  139.8 3.8 %reshape.233 = f32[18,12,2048]{2,1,0:T(8,128)} reshape(f32[18,12,2,2,512]{4,3,2,1,0:T(2,128)} %copy.45) | data formatting | bytes 3538944 | tf_op jit(solution)/shard_map/convert_element_type | solution.py:136
  143.6 4.3 %fusion.19 = bf16[18,12,1024]{2,1,0:T(8,128)(2,1)S(1)} fusion(bf16[2048,1024]{1,0:T(8,128)(2,1)} %param.14, f32[18,12,2048]{2,1,0:T(8,128)} %reshape.233, f32[18,12]{1,0:T(8,128)S(1)} %add_rsqrt_fusion.6, f32[18,12]{1,0:T(8,128)S(1)} %broadcast_multiply_fusion.2), kind=kOutput, calls=%fused_computation.26 | convolution fusion | flops 907517952 | bytes 6407872 | tf_op jit(solution)/shard_map/dot_general | solution.py:137
  (86 shorter events, 61.3 us)
Async XLA Ops:
  0.6 147.3 %copy-start = (bf16[1024,1536]{1,0:T(8,128)(2,1)S(1)}, bf16[1024,1536]{1,0:T(8,128)(2,1)}, u32[]{:S(2)}) copy-start(bf16[1024,1536]{1,0:T(8,128)(2,1)} %param.15) | copy-start | bytes 9437188
  4.0 1.5 copy-start.3
  6.8 33.3 %collective-permute-start = (bf16[36,6,1024]{2,0,1:T(8,128)(2,1)}, bf16[36,6,1024]{2,0,1:T(8,128)(2,1)}, u32[]{:S(2)}, u32[]{:S(2)}) collective-permute-start(bf16[36,6,1024]{2,0,1:T(8,128)(2,1)} %copy.33), channel_id=1, source_target_pairs={{0,2},{2,4},{4,6},{6,8},{8,10},{10,12},{12,14},{14,16},{16,18},{18... | collective-permute-start | bytes 1327112 | tf_op jit(solution)/shard_map/ppermute | solution.py:22
  8.3 10.0 %copy-start.8 = (s32[13,32]{1,0:T(8,128)S(1)}, s32[13,32]{1,0:T(8,128)}, u32[]{:S(2)}) copy-start(s32[13,32]{1,0:T(8,128)} %param.13) | copy-start | bytes 4996
  8.3 33.3 %collective-permute-start.1 = (bf16[36,6,1024]{2,0,1:T(8,128)(2,1)}, bf16[36,6,1024]{2,0,1:T(8,128)(2,1)}, u32[]{:S(2)}, u32[]{:S(2)}) collective-permute-start(bf16[36,6,1024]{2,0,1:T(8,128)(2,1)} %copy.34), channel_id=1, source_target_pairs={{2,0},{4,2},{6,4},{8,6},{10,8},{12,10},{14,12},{16,14},{18,16},{20... | collective-permute-start | bytes 1327112 | tf_op jit(solution)/shard_map/ppermute | solution.py:24
  40.0 2.8 %copy-start.2 = (bf16[36,24,1024]{2,1,0:T(8,128)(2,1)S(1)}, bf16[36,24,1024]{2,1,0:T(8,128)(2,1)}, u32[]{:S(2)}) copy-start(bf16[36,24,1024]{2,1,0:T(8,128)(2,1)} %slice.59) | copy-start | bytes 5308420
  43.0 7.5 %collective-permute-start.2 = (bf16[3,36,1024]{2,1,0:T(8,128)(2,1)S(1)}, bf16[3,36,1024]{2,1,0:T(8,128)(2,1)S(1)}, u32[]{:S(2)}, u32[]{:S(2)}) collective-permute-start(bf16[3,36,1024]{2,1,0:T(8,128)(2,1)S(1)} %get-tuple-element.4), channel_id=1, source_target_pairs={{0,1},{2,3},{4,5},{6,7},{8,9},{10,11},{12,13},{14,15},{16,17},{18,... | collective-permute-start | bytes 663560 | tf_op jit(solution)/shard_map/ppermute | solution.py:22
  46.9 8.1 %collective-permute-start.3 = (bf16[3,36,1024]{2,1,0:T(8,128)(2,1)S(1)}, bf16[3,36,1024]{2,1,0:T(8,128)(2,1)S(1)}, u32[]{:S(2)}, u32[]{:S(2)}) collective-permute-start(bf16[3,36,1024]{2,1,0:T(8,128)(2,1)S(1)} %get-tuple-element.5), channel_id=1, source_target_pairs={{1,0},{3,2},{5,4},{7,6},{9,8},{11,10},{13,12},{15,14},{17,16},{19,... | collective-permute-start | bytes 663560 | tf_op jit(solution)/shard_map/ppermute | solution.py:24
  92.8 5.5 %copy-start.10 = (f32[8]{0:T(128)S(1)}, f32[8]{0:T(128)}, u32[]{:S(2)}) copy-start(f32[8]{0:T(128)} %param.11) | copy-start | bytes 100
  98.3 5.4 %copy-start.4 = (bf16[21,72,1,8,64]{1,4,3,0,2:T(8,128)(2,1)S(1)}, bf16[21,72,1,8,64]{1,4,3,0,2:T(8,128)(2,1)}, u32[]{:S(2)}) copy-start(bf16[21,72,1,8,64]{1,4,3,0,2:T(8,128)(2,1)} %copy.79) | copy-start | bytes 4644868
  126.4 2.6 %copy-start.5 = (bf16[36,24,512]{2,1,0:T(8,128)(2,1)S(1)}, bf16[36,24,512]{2,1,0:T(8,128)(2,1)}, u32[]{:S(2)}) copy-start(bf16[36,24,512]{2,1,0:T(8,128)(2,1)} %param.9) | copy-start | bytes 2654212
  133.5 2.3 %copy-start.1 = (f32[18,2,12,2,512]{4,3,2,1,0:T(2,128)S(1)}, f32[18,2,12,2,512]{4,3,2,1,0:T(2,128)}, u32[]{:S(2)}) copy-start(f32[18,2,12,2,512]{4,3,2,1,0:T(2,128)} %reshape.235) | copy-start | bytes 5308420
  147.9 1.1 copy-start.6
  153.1 12.5 %copy-start.9 = (f32[8]{0:T(128)S(1)}, f32[8]{0:T(128)}, u32[]{:S(2)}) copy-start(f32[8]{0:T(128)} %param.16) | copy-start | bytes 100
  172.2 2.2 %copy-start.7 = (bf16[18,12,1024]{2,1,0:T(8,128)(2,1)S(1)}, bf16[18,12,1024]{2,1,0:T(8,128)(2,1)}, u32[]{:S(2)}) copy-start(bf16[18,12,1024]{2,1,0:T(8,128)(2,1)} %copy-done.6) | copy-start | bytes 1327108
where the time goes:
time: 177 us; the launch traced here: 175 us
  local copies, waits for them, and re-layouts  109 us (62%)
  matrix products  27.3 us (15%)
  other arithmetic  21.2 us (12%)
  starting transfers between devices  10.8 us (6%)
  waiting for transfers between devices  6.23 us (4%)
    unnamed x26, local copies, waits for them, and re-layouts  15.7 us
    reshape x2, local copies, waits for them, and re-layouts, to_windows(): grid.reshape(band_count, WLAT, col_count, WLON, grid.shape[-1])  9.78 us
    another operation x1, local copies, waits for them, and re-layouts, per_device(): win_kv = to_windows(border).reshape(win_count, place, 2, heads, head_dim)  9.68 us
    convert_element_type x3, local copies, waits for them, and re-layouts, per_device(): merge_in = layer_norm(quads.astype(jnp.float32)).astype(jnp.bfloat16)  9.48 us
    transpose x2, local copies, waits for them, and re-layouts, to_windows(): return grid.reshape(band_count, WLAT, col_count, WLON, grid.shape[-1]).tr...  8.1 us
    dot_general x2, matrix products, attend(): jnp.einsum('wqhe,wkhe->whqk', query, keys, preferred_element_type=jnp.flo...  7.85 us
    dot_general x2, matrix products, attend(): jnp.einsum('whqk,wkhe->wqhe', weights, values, preferred_element_type=jnp...  6.67 us
    ppermute x2, starting transfers between devices, extended(): lax.ppermute(head, axis, [((i + 1) % count, i) for i in range(ends)])  6.47 us
  transfers between devices with their start and end apart: 4, of which 2 were waited for; matrix products, arithmetic and copies ran while one was open for 17% of the time, Pallas kernels for 0%

commit v1 on v0

v1 whole, which is shorter than its diff:
```python
import functools
import math

import jax
import jax.numpy as jnp
import numpy as np
from jax import lax
from jax.experimental import pallas as pl
from jax.experimental.pallas import tpu as pltpu
from jax.sharding import PartitionSpec as P

WLAT = 6
WLON = 12
HEAD = 64
TILE = 8
LANES = 128
EPS_NORM = 1e-05
EPS_DIR = 1e-06
LOG2E = math.log2(math.e)
MESH = pl.DeviceIdType.MESH
BF16 = jnp.bfloat16
F32 = jnp.float32


def exchange_kernel(lat_count, lon_count, tokens, side, latr, send_sem, recv_sem):
    rows, blocks = tokens.shape[0], tokens.shape[1]
    half = WLAT // 2
    lat, lon = lax.axis_index("lat"), lax.axis_index("lon")
    south, north = lax.rem(lat + 1, lat_count), lax.rem(lat + lat_count - 1, lat_count)
    east, west = lax.rem(lon + 1, lon_count), lax.rem(lon + lon_count - 1, lon_count)
    last = blocks - 1
    top, bottom = pl.ds(0, half), pl.ds(rows - half, half)
    ext_top, ext_bottom, middle = pl.ds(0, half), pl.ds(rows + half, half), pl.ds(half, rows)
    plan = [
        ((lat, east), tokens.at[:, last], side.at[middle, 0]),
        ((lat, west), tokens.at[:, 0], side.at[middle, 1]),
        ((south, lon), tokens.at[bottom], latr.at[0]),
        ((north, lon), tokens.at[top], latr.at[1]),
        ((south, east), tokens.at[bottom, last], side.at[ext_top, 0]),
        ((north, east), tokens.at[top, last], side.at[ext_bottom, 0]),
        ((south, west), tokens.at[bottom, 0], side.at[ext_top, 1]),
        ((north, west), tokens.at[top, 0], side.at[ext_bottom, 1]),
    ]
    barrier = pltpu.get_barrier_semaphore()
    for (to_lat, to_lon), _, _ in plan:
        pl.semaphore_signal(
            barrier, inc=1, device_id={"lat": to_lat, "lon": to_lon}, device_id_type=MESH
        )
    pl.semaphore_wait(barrier, len(plan))
    copies = []
    for n, ((to_lat, to_lon), src, dst) in enumerate(plan):
        copy = pltpu.make_async_remote_copy(
            src_ref=src,
            dst_ref=dst,
            send_sem=send_sem.at[n],
            recv_sem=recv_sem.at[n],
            device_id={"lat": to_lat, "lon": to_lon},
            device_id_type=MESH,
        )
        copy.start()
        copies.append(copy)
    for copy in copies:
        copy.wait()


def exchange(tokens, lat_count, lon_count):
    rows, _, _, width = tokens.shape
    return pl.pallas_call(
        functools.partial(exchange_kernel, lat_count, lon_count),
        out_shape=(
            jax.ShapeDtypeStruct((rows + WLAT, 2, TILE, width), BF16),
            jax.ShapeDtypeStruct((2, WLAT // 2) + tokens.shape[1:], BF16),
        ),
        in_specs=[pl.BlockSpec(memory_space=pl.ANY)],
        out_specs=(pl.BlockSpec(memory_space=pl.ANY),) * 2,
        scratch_shapes=[pltpu.SemaphoreType.DMA((8,)), pltpu.SemaphoreType.DMA((8,))],
        compiler_params=pltpu.CompilerParams(collective_id=0, has_side_effects=True),
    )(tokens)


def normed(values):
    mean = jnp.mean(values, axis=-1, keepdims=True)
    centred = values - mean
    var = jnp.mean(centred * centred, axis=-1, keepdims=True)
    return centred * lax.rsqrt(var + EPS_NORM)


def dot(a, b):
    return jnp.dot(a, b, preferred_element_type=F32)


def directions(values, ones_block, scale_row):
    held = values.astype(BF16).astype(F32)
    squares = (held * held).astype(BF16)
    block = ones_block.shape[0]
    sums = jnp.concatenate(
        [dot(squares[:, s : s + block], ones_block) for s in range(0, values.shape[1], block)],
        axis=1,
    )
    unit = held * lax.rsqrt(sums + EPS_DIR)
    if scale_row is not None:
        unit = unit * scale_row
    return unit.astype(BF16)


def scale_lanes(scale, heads):
    lane = lax.broadcasted_iota(jnp.int32, (1, LANES), 1)
    return jnp.concatenate(
        [
            jnp.where(lane < HEAD, scale[h] * LOG2E, scale[h + 1] * LOG2E)
            for h in range(0, heads, 2)
        ],
        axis=1,
    )


def attend(query, keys, values, allowed):
    count = query.shape[0]
    lane = lax.broadcasted_iota(jnp.int32, (1, LANES), 1)
    low = (lane < HEAD).astype(F32).astype(BF16)
    high = (lane >= HEAD).astype(F32).astype(BF16)
    first = jnp.broadcast_to(lane < HEAD, (count, LANES))
    ones = jnp.ones((keys.shape[0], LANES), BF16)
    both = jnp.concatenate([allowed, allowed], axis=0)
    mixed = []
    for s in range(0, query.shape[1], LANES):
        pair = query[:, s : s + LANES]
        stacked = jnp.concatenate([pair * low, pair * high], axis=0)
        score = lax.dot_general(
            stacked, keys[:, s : s + LANES], (((1,), (1,)), ((), ())), preferred_element_type=F32
        )
        expo = (jnp.exp2(score) * both).astype(BF16)
        out = dot(expo, jnp.concatenate([values[:, s : s + LANES], ones], axis=1))
        top = jnp.where(first, out[:count, :LANES], out[count:, :LANES])
        total = jnp.where(first, out[:count, LANES:], out[count:, LANES:])
        mixed.append(top / total)
    return jnp.concatenate(mixed, axis=1)


def body_kernel(
    lat_count,
    fine_scale,
    mid_scale,
    window_mask,
    q_static,
    k_static,
    mid_q,
    mid_k,
    ones_block,
    perm,
    spread,
    tokens,
    side,
    latr,
    fine_qkv,
    fine_proj,
    merge_weight,
    mid_qkv,
    mid_proj,
    fine_out,
    mid_out,
    core,
    halo,
    w_qkv,
    w_proj,
    w_merge,
    w_mqkv,
    w_mproj,
    mix,
    out_buf,
    sem,
    out_sem,
):
    rows, blocks, _, width = tokens.shape
    half = WLAT // 2
    cols = blocks * TILE
    bands = (rows + WLAT) // WLAT
    loads = [
        pltpu.make_async_copy(src, dst, sem.at[n])
        for n, (src, dst) in enumerate(
            [
                (tokens, core.at[pl.ds(half, rows)]),
                (latr.at[0], core.at[pl.ds(0, half)]),
                (latr.at[1], core.at[pl.ds(rows + half, half)]),
                (side, halo),
                (fine_qkv, w_qkv),
                (fine_proj, w_proj),
                (merge_weight, w_merge),
                (mid_qkv, w_mqkv),
                (mid_proj, w_mproj),
            ]
        )
    ]
    for load in loads:
        load.start()
    lat, lon = lax.axis_index("lat"), lax.axis_index("lon")
    fine_row = scale_lanes(fine_scale, width // HEAD)
    q_win, q_lat, q_lon = q_static[:, 0:1], q_static[:, 1:2], q_static[:, 2:3]
    k_win, k_lat, k_lon = k_static[0:1], k_static[1:2], k_static[2:3]
    per_row = window_mask.shape[1]
    blocks_of = ones_block[...]
    for load in loads[:5]:
        load.wait()

    def band_step(b, carry):
        x_core = core[pl.ds(b * WLAT, WLAT)].astype(F32).reshape(WLAT * cols, width).astype(BF16)
        x_halo = (
            halo[pl.ds(b * WLAT, WLAT)].astype(F32).reshape(WLAT * 2 * TILE, width).astype(BF16)
        )
        x_all = jnp.concatenate([x_core, x_halo], axis=0)
        query = directions(dot(x_core, w_qkv[:, :width]), blocks_of, fine_row)
        keys = directions(dot(x_all, w_qkv[:, width : 2 * width]), blocks_of, None)
        values = dot(x_all, w_qkv[:, 2 * width :]).astype(BF16)
        q_code, k_code = q_win * 4, k_win * 4
        for w in range(cols // WLON + 1):
            column = lax.rem(lon * (cols // WLON) + w - 1 + per_row, per_row)
            pattern = window_mask[lat * (rows // WLAT) + b, column]
            by_lat, by_lon = (pattern & 1) * 2, (pattern >> 1) & 1
            q_code = q_code + jnp.where(q_win == w, q_lat * by_lat + q_lon * by_lon, 0)
            k_code = k_code + jnp.where(k_win == w, k_lat * by_lat + k_lon * by_lon, 0)
        no_north = (lat == 0) & (b == 0)
        no_south = (lat == lat_count - 1) & (b == bands - 1)
        gone_low = jnp.where(no_north, 1, 0)
        gone_high = jnp.where(no_south, 1, 0)
        gone = (1 - k_lat) * gone_low + k_lat * gone_high
        k_code = jnp.where((gone > 0) | (k_win < 0), -1, k_code)
        allowed = jnp.where(q_code == k_code, 1.0, 0.0).astype(F32)
        mix[b] = attend(query, keys, values, allowed)
        return carry

    lax.fori_loop(0, bands, band_step, 0)

    for load in loads[5:]:
        load.wait()
    chunk = 2 * WLAT
    size = chunk * cols
    merged_in = []
    flat = mix[...].reshape(bands * WLAT * cols, width)
    for c in range(rows // chunk):
        start = half * cols + c * size
        x = core[pl.ds(half + c * chunk, chunk)].astype(F32).reshape(size, width)
        projected = dot(flat[start : start + size].astype(BF16), w_proj[...])
        result = x + normed(projected)
        out_buf[pl.ds(c * chunk, chunk)] = result.reshape(chunk, blocks, TILE, width).astype(BF16)
        moved = dot(perm[...], result.astype(BF16))
        quarter = size // 4
        quads = jnp.concatenate(
            [moved[g * quarter : (g + 1) * quarter] for g in range(4)], axis=1
        )
        merged_in.append(normed(quads))
    fine_copy = pltpu.make_async_copy(out_buf, fine_out, out_sem)
    fine_copy.start()
    merge_in = jnp.concatenate(merged_in, axis=0).astype(BF16)
    merged = dot(merge_in, w_merge[...]).astype(BF16)
    mid_width = mid_proj.shape[0]
    act = dot(merged, w_mqkv[...])
    mid_row = scale_lanes(mid_scale, mid_width // HEAD)
    query = directions(act[:, :mid_width], blocks_of, mid_row)
    keys = directions(act[:, mid_width : 2 * mid_width], blocks_of, None)
    values = act[:, 2 * mid_width :].astype(BF16)
    allowed = jnp.where(mid_q[...] == mid_k[...], 1.0, 0.0).astype(F32)
    mid_mix = attend(query, keys, values, allowed).astype(BF16)
    mid_result = (merged.astype(F32) + normed(dot(mid_mix, w_mproj[...]))).astype(BF16)
    wide = dot(spread[...], mid_result).reshape(rows // 2, 2 * TILE, mid_result.shape[1])
    mid_out[...] = wide[:, : cols // 2].astype(BF16)
    fine_copy.wait()


def statics(rows, cols):
    half_lat, half_lon = WLAT // 2, WLON // 2
    i, c = np.divmod(np.arange(WLAT * cols), cols)
    core = np.stack(
        [(c + half_lon) // WLON, i >= half_lat, (c + half_lon) % WLON >= half_lon]
    ).astype(np.int32)
    i, m = np.divmod(np.arange(WLAT * 2 * TILE), 2 * TILE)
    west = m < TILE
    real = np.where(west, m >= TILE - half_lon, m < TILE + half_lon)
    window = np.where(west, 0, cols // WLON)
    halo = np.stack([np.where(real, window, -1), i >= half_lat, ~west]).astype(np.int32)
    k_static = np.concatenate([core, halo], axis=1)
    coarse_rows, coarse_cols = rows // 2, cols // 2
    tokens = np.arange(coarse_rows * coarse_cols)
    r, c = np.divmod(tokens, coarse_cols)
    mid = ((r // WLAT) * (coarse_cols // WLON) + c // WLON).astype(np.int32)
    block = np.kron(np.eye(4, dtype=np.float32), np.ones((HEAD, HEAD), np.float32))
    size = 2 * WLAT * cols
    perm = np.zeros((size, size), np.float32)
    out = np.arange(size)
    g, rest = np.divmod(out, size // 4)
    r, s = np.divmod(rest, coarse_cols)
    perm[out, (2 * r + g % 2) * cols + 2 * s + g // 2] = 1.0
    spread = np.zeros((coarse_rows * 2 * TILE, coarse_rows * coarse_cols), np.float32)
    r, c = np.divmod(tokens, coarse_cols)
    spread[r * 2 * TILE + c, tokens] = 1.0
    return (
        jnp.asarray(core.T),
        jnp.asarray(k_static),
        jnp.asarray(mid[:, None]),
        jnp.asarray(mid[None, :]),
        jnp.asarray(block, BF16),
        jnp.asarray(perm, BF16),
        jnp.asarray(spread, BF16),
    )


def per_device(
    lat_count,
    lon_count,
    fine_tokens,
    fine_qkv,
    fine_scale,
    fine_proj,
    window_mask,
    merge_weight,
    mid_qkv,
    mid_scale,
    mid_proj,
):
    rows, cols, width = fine_tokens.shape
    blocks = cols // TILE
    tokens = fine_tokens.reshape(rows, blocks, TILE, width)
    side, latr = exchange(tokens, lat_count, lon_count)
    smem = pl.BlockSpec(memory_space=pltpu.SMEM)
    vmem = pl.BlockSpec(memory_space=pltpu.VMEM)
    anywhere = pl.BlockSpec(memory_space=pl.ANY)
    weights = (fine_qkv, fine_proj, merge_weight, mid_qkv, mid_proj)
    bands = (rows + WLAT) // WLAT
    fine_out, mid_out = pl.pallas_call(
        functools.partial(body_kernel, lat_count),
        out_shape=(
            jax.ShapeDtypeStruct(tokens.shape, BF16),
            jax.ShapeDtypeStruct((rows // 2, cols // 2, merge_weight.shape[1]), BF16),
        ),
        in_specs=[smem] * 3 + [vmem] * 7 + [anywhere] * 8,
        out_specs=(anywhere, vmem),
        scratch_shapes=[
            pltpu.VMEM((rows + WLAT,) + tokens.shape[1:], BF16),
            pltpu.VMEM(side.shape, BF16),
        ]
        + [pltpu.VMEM(w.shape, BF16) for w in weights]
        + [
            pltpu.VMEM((bands, WLAT * cols, width), F32),
            pltpu.VMEM(tokens.shape, BF16),
            pltpu.SemaphoreType.DMA((9,)),
            pltpu.SemaphoreType.DMA,
        ],
        compiler_params=pltpu.CompilerParams(vmem_limit_bytes=50 * 1024 * 1024),
    )(
        fine_scale,
        mid_scale,
        window_mask,
        *statics(rows, cols),
        tokens,
        side,
        latr,
        *weights,
    )
    return fine_out.reshape(rows, cols, width), mid_out


def solution(mesh):
    return jax.shard_map(
        functools.partial(per_device, mesh.shape["lat"], mesh.shape["lon"]),
        mesh=mesh,
        in_specs=(P("lat", "lon", None), P(), P(), P(), P(), P(), P(), P(), P()),
        out_specs=(P("lat", "lon", None), P("lat", "lon", None)),
        check_vma=False,
    )
```

time: 177 us -> 46.7 us (0.26)
  local copies, waits for them, and re-layouts: 109 us -> 13.3 us
  Pallas kernels: 0 us -> 32.2 us
  matrix products: 27.3 us -> 0 us
  other arithmetic: 21.2 us -> 0 us
  starting transfers between devices: 10.8 us -> 0 us
  waiting for transfers between devices: 6.23 us -> 0 us
    pallas_call x0 -> x2, Pallas kernels: none -> 32.2 us  [the longest x1 18.8 us: per_device(): pl.pallas_call(functools.partial(body_kernel, lat_count), out_shape=(jax....]
    dot_general x9 -> x0, matrix products: 27.3 us -> none  [the longest x2 7.85 us: attend(): jnp.einsum('wqhe,wkhe->whqk', query, keys, preferred_element_type=jnp.flo...]
    reshape x8 -> x0, local copies, waits for them, and re-layouts: 25 us -> none  [the longest x2 9.78 us: to_windows(): grid.reshape(band_count, WLAT, col_count, WLON, grid.shape[-1])]
    slice x10 -> x0, local copies, waits for them, and re-layouts: 16.9 us -> none  [the longest x1 5.85 us: per_device(): win_kv[:, :, 1]]
    convert_element_type x5 -> x0, local copies, waits for them, and re-layouts: 15.9 us -> none  [the longest x3 9.48 us: per_device(): merge_in = layer_norm(quads.astype(jnp.float32)).astype(jnp.bfloat16)]
    another operation x2 -> x0, local copies, waits for them, and re-layouts: 15.2 us -> none  [the longest x1 9.68 us: per_device(): win_kv = to_windows(border).reshape(win_count, place, 2, heads, head_dim)]
    transpose x3 -> x0, local copies, waits for them, and re-layouts: 11.2 us -> none  [the longest x2 8.1 us: to_windows(): return grid.reshape(band_count, WLAT, col_count, WLON, grid.shape[-1]).tr...]
    ppermute x4 -> x0, starting transfers between devices: 10.8 us -> none  [the longest x2 6.47 us: extended(): lax.ppermute(head, axis, [((i + 1) % count, i) for i in range(ends)])]
  transfers between devices with their start and end apart: 4 -> 0, of which waited for: 2 -> 0; matrix products, arithmetic and copies ran while one was open for 17% -> 0% of each run, Pallas kernels for 0% -> 0%
where the time goes in v1:
time: 46.7 us; the launch traced here: 46.2 us
  Pallas kernels  32.2 us (69%)
  local copies, waits for them, and re-layouts  13.3 us (28%)
  between operations  0.66 us (1%)
    pallas_call x1, Pallas kernels, per_device(): pl.pallas_call(functools.partial(body_kernel, lat_count), out_shape=(jax....  18.8 us
    pallas_call x1, Pallas kernels, exchange(): pl.pallas_call(functools.partial(exchange_kernel, lat_count, lon_count),...  13.4 us
    unnamed x30, local copies, waits for them, and re-layouts  13.3 us

profile of v1, /device:TPU:0, one launch (start us, length us, event | category | flops | bytes accessed | tf_op | source)
XLA Modules:
  0.0 46.2 jit_solution(1558360516636852264)
XLA Ops:
  0.6 13.4 %shard_map.167 = (bf16[42,2,8,512]{3,2,1,0:T(8,128)(2,1)}, bf16[2,3,3,8,512]{4,3,2,1,0:T(8,128)(2,1)}) custom-call(bf16[36,3,8,512]{3,2,1,0:T(8,128)(2,1)} %bitcast.2), custom_call_target="tpu_custom_call" | custom-call | tf_op jit(solution)/shard_map/pallas_call | solution.py:68
  14.0 0.0 copy-start
  14.0 1.2 %copy-done = bf16[36,24,512]{2,1,0:T(8,128)(2,1)S(1)} copy-done((bf16[36,24,512]{2,1,0:T(8,128)(2,1)S(1)}, bf16[36,24,512]{2,1,0:T(8,128)(2,1)}, u32[]{:S(2)}) %copy-start) | copy-done | bytes 884760
  15.2 0.0 copy-start.1
  15.2 1.2 %copy-done.1 = bf16[512,1024]{1,0:T(8,128)(2,1)S(1)} copy-done((bf16[512,1024]{1,0:T(8,128)(2,1)S(1)}, bf16[512,1024]{1,0:T(8,128)(2,1)}, u32[]{:S(2)}) %copy-start.1) | copy-done | bytes 1048600
  16.4 0.0 copy-start.2
  16.4 1.1 %copy-done.2 = bf16[42,2,8,512]{3,2,1,0:T(8,128)(2,1)S(1)} copy-done((bf16[42,2,8,512]{3,2,1,0:T(8,128)(2,1)S(1)}, bf16[42,2,8,512]{3,2,1,0:T(8,128)(2,1)}, u32[]{:S(2)}) %copy-start.2) | copy-done | bytes 688152
  17.5 0.0 copy-start.3
  17.5 1.0 %copy-done.3 = bf16[512,512]{1,0:T(8,128)(2,1)S(1)} copy-done((bf16[512,512]{1,0:T(8,128)(2,1)S(1)}, bf16[512,512]{1,0:T(8,128)(2,1)}, u32[]{:S(2)}) %copy-start.3) | copy-done | bytes 524312
  18.5 0.0 copy-start.4
  18.5 0.9 %copy-done.4 = bf16[288,288]{1,0:T(8,128)(2,1)S(1)} copy-done((bf16[288,288]{1,0:T(8,128)(2,1)S(1)}, bf16[288,288]{1,0:T(8,128)(2,1)}, u32[]{:S(2)}) %copy-start.4) | copy-done | bytes 165912
  19.5 0.0 copy-start.5
  19.5 0.9 %copy-done.5 = bf16[288,216]{1,0:T(8,128)(2,1)S(1)} copy-done((bf16[288,216]{1,0:T(8,128)(2,1)S(1)}, bf16[288,216]{1,0:T(8,128)(2,1)}, u32[]{:S(2)}) %copy-start.5) | copy-done | bytes 124440
  20.4 0.9 %copy-done.6 = bf16[2,3,3,8,512]{4,3,2,1,0:T(8,128)(2,1)S(1)} copy-done((bf16[2,3,3,8,512]{4,3,2,1,0:T(8,128)(2,1)S(1)}, bf16[2,3,3,8,512]{4,3,2,1,0:T(8,128)(2,1)}, u32[]{:S(2)}) %copy-start.6) | copy-done | bytes 147480
  21.3 0.0 copy-start.7
  21.3 0.9 %copy-done.7 = bf16[256,256]{1,0:T(8,128)(2,1)S(1)} copy-done((bf16[256,256]{1,0:T(8,128)(2,1)S(1)}, bf16[256,256]{1,0:T(8,128)(2,1)}, u32[]{:S(2)}) %copy-start.7) | copy-done | bytes 131096
  22.2 0.9 %copy-done.8 = s32[216,1]{1,0:T(8,128)S(1)} copy-done((s32[216,1]{1,0:T(8,128)S(1)}, s32[216,1]{1,0:T(8,128)}, u32[]{:S(2)}) %copy-start.8) | copy-done | bytes 888
  23.1 0.9 %copy-done.9 = s32[144,3]{1,0:T(8,128)S(1)} copy-done((s32[144,3]{1,0:T(8,128)S(1)}, s32[144,3]{1,0:T(8,128)}, u32[]{:S(2)}) %copy-start.9) | copy-done | bytes 1752
  24.0 0.7 %copy-done.10 = s32[13,32]{1,0:T(8,128)S(1)} copy-done((s32[13,32]{1,0:T(8,128)S(1)}, s32[13,32]{1,0:T(8,128)}, u32[]{:S(2)}) %copy-start.10) | copy-done | bytes 1688
  24.7 0.7 %copy-done.11 = s32[3,240]{1,0:T(4,128)S(1)} copy-done((s32[3,240]{1,0:T(4,128)S(1)}, s32[3,240]{1,0:T(4,128)}, u32[]{:S(2)}) %copy-start.11) | copy-done | bytes 2904
  25.4 0.7 %copy-done.12 = s32[1,216]{1,0:T(1,128)S(1)} copy-done((s32[1,216]{1,0:T(1,128)S(1)}, s32[1,216]{1,0:T(1,128)}, u32[]{:S(2)}) %copy-start.12) | copy-done | bytes 888
  26.1 0.7 %copy-done.13 = f32[8]{0:T(128)S(1)} copy-done((f32[8]{0:T(128)S(1)}, f32[8]{0:T(128)}, u32[]{:S(2)}) %copy-start.13) | copy-done | bytes 56
  26.7 0.7 %copy-done.14 = f32[8]{0:T(128)S(1)} copy-done((f32[8]{0:T(128)S(1)}, f32[8]{0:T(128)}, u32[]{:S(2)}) %copy-start.14) | copy-done | bytes 56
  27.4 18.8 %shard_map.168 = (bf16[36,3,8,512]{3,2,1,0:T(8,128)(2,1)}, bf16[18,12,1024]{2,1,0:T(8,128)(2,1)}) custom-call(f32[8]{0:T(128)S(1)} %copy-done.13, f32[8]{0:T(128)S(1)} %copy-done.14, s32[13,32]{1,0:T(8,128)S(1)} %copy-done.10, s32[144,3]{1,0:T(8,128)S(1)} %copy-done.9, s32[3,240]{1,0:T(4,128)S(1)} %copy-done.11, s32[216,1]{1,0:T(8,128)S(1)} %copy-done.8, ...), custom_call_target="tpu_custom_call" | custom-call | tf_op jit(solution)/shard_map/pallas_call | solution.py:328
  (8 shorter events, 0.0 us)
Async XLA Ops:
  14.0 1.2 %copy-start = (bf16[36,24,512]{2,1,0:T(8,128)(2,1)S(1)}, bf16[36,24,512]{2,1,0:T(8,128)(2,1)}, u32[]{:S(2)}) copy-start(bf16[36,24,512]{2,1,0:T(8,128)(2,1)} %param.16) | copy-start | bytes 2654212
  15.2 1.2 %copy-start.1 = (bf16[512,1024]{1,0:T(8,128)(2,1)S(1)}, bf16[512,1024]{1,0:T(8,128)(2,1)}, u32[]{:S(2)}) copy-start(bf16[512,1024]{1,0:T(8,128)(2,1)} %mid_proj.1) | copy-start | bytes 3145732
  16.4 1.1 %copy-start.2 = (bf16[42,2,8,512]{3,2,1,0:T(8,128)(2,1)S(1)}, bf16[42,2,8,512]{3,2,1,0:T(8,128)(2,1)}, u32[]{:S(2)}) copy-start(bf16[42,2,8,512]{3,2,1,0:T(8,128)(2,1)} %get-tuple-element.6.side) | copy-start | bytes 2064388
  17.5 1.0 %copy-start.3 = (bf16[512,512]{1,0:T(8,128)(2,1)S(1)}, bf16[512,512]{1,0:T(8,128)(2,1)}, u32[]{:S(2)}) copy-start(bf16[512,512]{1,0:T(8,128)(2,1)} %fine_proj.1) | copy-start | bytes 1572868
  18.5 0.9 %copy-start.4 = (bf16[288,288]{1,0:T(8,128)(2,1)S(1)}, bf16[288,288]{1,0:T(8,128)(2,1)}, u32[]{:S(2)}) copy-start(bf16[288,288]{1,0:T(8,128)(2,1)} %constant.19.clone.perm) | copy-start | bytes 497668
  19.5 0.9 %copy-start.5 = (bf16[288,216]{1,0:T(8,128)(2,1)S(1)}, bf16[288,216]{1,0:T(8,128)(2,1)}, u32[]{:S(2)}) copy-start(bf16[288,216]{1,0:T(8,128)(2,1)} %constant.20.clone.spread) | copy-start | bytes 373252
  20.4 0.9 %copy-start.6 = (bf16[2,3,3,8,512]{4,3,2,1,0:T(8,128)(2,1)S(1)}, bf16[2,3,3,8,512]{4,3,2,1,0:T(8,128)(2,1)}, u32[]{:S(2)}) copy-start(bf16[2,3,3,8,512]{4,3,2,1,0:T(8,128)(2,1)} %get-tuple-element.7.latr) | copy-start | bytes 442372
  21.3 0.9 %copy-start.7 = (bf16[256,256]{1,0:T(8,128)(2,1)S(1)}, bf16[256,256]{1,0:T(8,128)(2,1)}, u32[]{:S(2)}) copy-start(bf16[256,256]{1,0:T(8,128)(2,1)} %constant.18.clone.ones_block) | copy-start | bytes 393220
  22.2 0.9 %copy-start.8 = (s32[216,1]{1,0:T(8,128)S(1)}, s32[216,1]{1,0:T(8,128)}, u32[]{:S(2)}) copy-start(s32[216,1]{1,0:T(8,128)} %constant.16.clone.mid_q) | copy-start | bytes 2596
  23.1 0.9 %copy-start.9 = (s32[144,3]{1,0:T(8,128)S(1)}, s32[144,3]{1,0:T(8,128)}, u32[]{:S(2)}) copy-start(s32[144,3]{1,0:T(8,128)} %constant.14.clone.q_static) | copy-start | bytes 5188
  24.0 0.7 %copy-start.10 = (s32[13,32]{1,0:T(8,128)S(1)}, s32[13,32]{1,0:T(8,128)}, u32[]{:S(2)}) copy-start(s32[13,32]{1,0:T(8,128)} %window_mask.1) | copy-start | bytes 4996
  24.7 0.7 %copy-start.11 = (s32[3,240]{1,0:T(4,128)S(1)}, s32[3,240]{1,0:T(4,128)}, u32[]{:S(2)}) copy-start(s32[3,240]{1,0:T(4,128)} %constant.15.clone.k_static) | copy-start | bytes 8644
  25.4 0.7 %copy-start.12 = (s32[1,216]{1,0:T(1,128)S(1)}, s32[1,216]{1,0:T(1,128)}, u32[]{:S(2)}) copy-start(s32[1,216]{1,0:T(1,128)} %constant.17.clone.mid_k) | copy-start | bytes 2596
  26.0 0.7 %copy-start.13 = (f32[8]{0:T(128)S(1)}, f32[8]{0:T(128)}, u32[]{:S(2)}) copy-start(f32[8]{0:T(128)} %fine_scale.1) | copy-start | bytes 100
  26.7 0.7 %copy-start.14 = (f32[8]{0:T(128)S(1)}, f32[8]{0:T(128)}, u32[]{:S(2)}) copy-start(f32[8]{0:T(128)} %mid_scale.1) | copy-start | bytes 100

commit v2 on v1

--- a/solution.py
+++ b/solution.py
@@ -22,7 +22,7 @@
 F32 = jnp.float32
 
 
-def exchange_kernel(lat_count, lon_count, tokens, side, latr, send_sem, recv_sem):
+def sends(lat_count, lon_count, tokens, core, halo, send_sem, recv_sem):
     rows, blocks = tokens.shape[0], tokens.shape[1]
     half = WLAT // 2
     lat, lon = lax.axis_index("lat"), lax.axis_index("lon")
@@ -30,52 +30,31 @@
     east, west = lax.rem(lon + 1, lon_count), lax.rem(lon + lon_count - 1, lon_count)
     last = blocks - 1
     top, bottom = pl.ds(0, half), pl.ds(rows - half, half)
-    ext_top, ext_bottom, middle = pl.ds(0, half), pl.ds(rows + half, half), pl.ds(half, rows)
+    below, middle = pl.ds(rows + half, half), pl.ds(half, rows)
     plan = [
-        ((lat, east), tokens.at[:, last], side.at[middle, 0]),
-        ((lat, west), tokens.at[:, 0], side.at[middle, 1]),
-        ((south, lon), tokens.at[bottom], latr.at[0]),
-        ((north, lon), tokens.at[top], latr.at[1]),
-        ((south, east), tokens.at[bottom, last], side.at[ext_top, 0]),
-        ((north, east), tokens.at[top, last], side.at[ext_bottom, 0]),
-        ((south, west), tokens.at[bottom, 0], side.at[ext_top, 1]),
-        ((north, west), tokens.at[top, 0], side.at[ext_bottom, 1]),
+        ((lat, east), tokens.at[:, last], halo.at[middle, 0]),
+        ((lat, west), tokens.at[:, 0], halo.at[middle, 1]),
+        ((south, lon), tokens.at[bottom], core.at[top]),
+        ((north, lon), tokens.at[top], core.at[below]),
+        ((south, east), tokens.at[bottom, last], halo.at[top, 0]),
+        ((north, east), tokens.at[top, last], halo.at[below, 0]),
+        ((south, west), tokens.at[bottom, 0], halo.at[top, 1]),
+        ((north, west), tokens.at[top, 0], halo.at[below, 1]),
     ]
-    barrier = pltpu.get_barrier_semaphore()
-    for (to_lat, to_lon), _, _ in plan:
-        pl.semaphore_signal(
-            barrier, inc=1, device_id={"lat": to_lat, "lon": to_lon}, device_id_type=MESH
+    return [
+        (
+            {"lat": to_lat, "lon": to_lon},
+            pltpu.make_async_remote_copy(
+                src_ref=src,
+                dst_ref=dst,
+                send_sem=send_sem.at[n],
+                recv_sem=recv_sem.at[n],
+                device_id={"lat": to_lat, "lon": to_lon},
+                device_id_type=MESH,
+            ),
         )
-    pl.semaphore_wait(barrier, len(plan))
-    copies = []
-    for n, ((to_lat, to_lon), src, dst) in enumerate(plan):
-        copy = pltpu.make_async_remote_copy(
-            src_ref=src,
-            dst_ref=dst,
-            send_sem=send_sem.at[n],
-            recv_sem=recv_sem.at[n],
-            device_id={"lat": to_lat, "lon": to_lon},
-            device_id_type=MESH,
-        )
-        copy.start()
-        copies.append(copy)
-    for copy in copies:
-        copy.wait()
-
-
-def exchange(tokens, lat_count, lon_count):
-    rows, _, _, width = tokens.shape
-    return pl.pallas_call(
-        functools.partial(exchange_kernel, lat_count, lon_count),
-        out_shape=(
-            jax.ShapeDtypeStruct((rows + WLAT, 2, TILE, width), BF16),
-            jax.ShapeDtypeStruct((2, WLAT // 2) + tokens.shape[1:], BF16),
-        ),
-        in_specs=[pl.BlockSpec(memory_space=pl.ANY)],
-        out_specs=(pl.BlockSpec(memory_space=pl.ANY),) * 2,
-        scratch_shapes=[pltpu.SemaphoreType.DMA((8,)), pltpu.SemaphoreType.DMA((8,))],
-        compiler_params=pltpu.CompilerParams(collective_id=0, has_side_effects=True),
-    )(tokens)
+        for n, ((to_lat, to_lon), src, dst) in enumerate(plan)
+    ]
 
 
 def normed(values):
@@ -139,19 +118,18 @@
 
 def body_kernel(
     lat_count,
+    lon_count,
     fine_scale,
     mid_scale,
     window_mask,
-    q_static,
-    k_static,
-    mid_q,
-    mid_k,
-    ones_block,
-    perm,
-    spread,
+    q_static_hbm,
+    k_static_hbm,
+    mid_q_hbm,
+    mid_k_hbm,
+    block_hbm,
+    perm_hbm,
+    spread_hbm,
     tokens,
-    side,
-    latr,
     fine_qkv,
     fine_proj,
     merge_weight,
@@ -161,56 +139,104 @@
     mid_out,
     core,
     halo,
+    q_static,
+    k_static,
+    mid_q,
+    mid_k,
+    ones_block,
+    perm,
+    spread,
     w_qkv,
     w_proj,
     w_merge,
     w_mqkv,
     w_mproj,
+    q_s,
+    k_s,
+    v_s,
     mix,
     out_buf,
     sem,
     out_sem,
+    send_sem,
+    recv_sem,
 ):
     rows, blocks, _, width = tokens.shape
     half = WLAT // 2
     cols = blocks * TILE
     bands = (rows + WLAT) // WLAT
+    place = WLAT * cols
+    beside = WLAT * 2 * TILE
+    copies = sends(lat_count, lon_count, tokens, core, halo, send_sem, recv_sem)
+    barrier = pltpu.get_barrier_semaphore()
+    for device, _ in copies:
+        pl.semaphore_signal(barrier, inc=1, device_id=device, device_id_type=MESH)
     loads = [
         pltpu.make_async_copy(src, dst, sem.at[n])
         for n, (src, dst) in enumerate(
             [
                 (tokens, core.at[pl.ds(half, rows)]),
-                (latr.at[0], core.at[pl.ds(0, half)]),
-                (latr.at[1], core.at[pl.ds(rows + half, half)]),
-                (side, halo),
                 (fine_qkv, w_qkv),
+                (block_hbm, ones_block),
+                (q_static_hbm, q_static),
+                (k_static_hbm, k_static),
                 (fine_proj, w_proj),
+                (perm_hbm, perm),
                 (merge_weight, w_merge),
                 (mid_qkv, w_mqkv),
+                (mid_q_hbm, mid_q),
+                (mid_k_hbm, mid_k),
                 (mid_proj, w_mproj),
+                (spread_hbm, spread),
             ]
         )
     ]
     for load in loads:
         load.start()
+    pl.semaphore_wait(barrier, len(copies))
+    for _, copy in copies:
+        copy.start()
     lat, lon = lax.axis_index("lat"), lax.axis_index("lon")
     fine_row = scale_lanes(fine_scale, width // HEAD)
+    for load in loads[:5]:
+        load.wait()
+    blocks_of = ones_block[...].astype(BF16)
+
+    def rows_of(ref, first, count):
+        part = ref[pl.ds(first, count)]
+        return part.astype(F32).reshape(part.shape[0] * part.shape[1] * TILE, width).astype(BF16)
+
+    def query_of(x):
+        return directions(dot(x, w_qkv[:, :width]), blocks_of, fine_row)
+
+    def keys_of(x):
+        return directions(dot(x, w_qkv[:, width : 2 * width]), blocks_of, None)
+
+    def values_of(x):
+        return dot(x, w_qkv[:, 2 * width :]).astype(BF16)
+
+    inner = bands - 2
+    own = rows_of(core, WLAT, inner * WLAT)
+    q_s[pl.ds(1, inner)] = query_of(own).reshape(inner, place, width)
+    k_s[pl.ds(1, inner), pl.ds(0, place)] = keys_of(own).reshape(inner, place, width)
+    v_s[pl.ds(1, inner), pl.ds(0, place)] = values_of(own).reshape(inner, place, width)
+    for _, copy in copies:
+        copy.wait_recv()
+    ends = jnp.concatenate(
+        [rows_of(core, 0, WLAT), rows_of(core, rows, WLAT), rows_of(halo, 0, rows + WLAT)], axis=0
+    )
+    query = query_of(ends[: 2 * place])
+    for target, found in ((k_s, keys_of(ends)), (v_s, values_of(ends))):
+        target[0, pl.ds(0, place)] = found[:place]
+        target[bands - 1, pl.ds(0, place)] = found[place : 2 * place]
+        target[:, pl.ds(place, beside)] = found[2 * place :].reshape(bands, beside, width)
+    q_s[0] = query[:place]
+    q_s[bands - 1] = query[place:]
     q_win, q_lat, q_lon = q_static[:, 0:1], q_static[:, 1:2], q_static[:, 2:3]
     k_win, k_lat, k_lon = k_static[0:1], k_static[1:2], k_static[2:3]
     per_row = window_mask.shape[1]
-    blocks_of = ones_block[...]
-    for load in loads[:5]:
-        load.wait()
 
     def band_step(b, carry):
-        x_core = core[pl.ds(b * WLAT, WLAT)].astype(F32).reshape(WLAT * cols, width).astype(BF16)
-        x_halo = (
-            halo[pl.ds(b * WLAT, WLAT)].astype(F32).reshape(WLAT * 2 * TILE, width).astype(BF16)
-        )
-        x_all = jnp.concatenate([x_core, x_halo], axis=0)
-        query = directions(dot(x_core, w_qkv[:, :width]), blocks_of, fine_row)
-        keys = directions(dot(x_all, w_qkv[:, width : 2 * width]), blocks_of, None)
-        values = dot(x_all, w_qkv[:, 2 * width :]).astype(BF16)
         q_code, k_code = q_win * 4, k_win * 4
         for w in range(cols // WLON + 1):
             column = lax.rem(lon * (cols // WLON) + w - 1 + per_row, per_row)
@@ -225,13 +251,14 @@
         gone = (1 - k_lat) * gone_low + k_lat * gone_high
         k_code = jnp.where((gone > 0) | (k_win < 0), -1, k_code)
         allowed = jnp.where(q_code == k_code, 1.0, 0.0).astype(F32)
-        mix[b] = attend(query, keys, values, allowed)
+        mix[b] = attend(q_s[b], k_s[b], v_s[b], allowed)
         return carry
 
     lax.fori_loop(0, bands, band_step, 0)
 
     for load in loads[5:]:
         load.wait()
+    mover = perm[...].astype(BF16)
     chunk = 2 * WLAT
     size = chunk * cols
     merged_in = []
@@ -242,7 +269,7 @@
         projected = dot(flat[start : start + size].astype(BF16), w_proj[...])
         result = x + normed(projected)
         out_buf[pl.ds(c * chunk, chunk)] = result.reshape(chunk, blocks, TILE, width).astype(BF16)
-        moved = dot(perm[...], result.astype(BF16))
+        moved = dot(mover, result.astype(BF16))
         quarter = size // 4
         quads = jnp.concatenate(
             [moved[g * quarter : (g + 1) * quarter] for g in range(4)], axis=1
@@ -261,9 +288,11 @@
     allowed = jnp.where(mid_q[...] == mid_k[...], 1.0, 0.0).astype(F32)
     mid_mix = attend(query, keys, values, allowed).astype(BF16)
     mid_result = (merged.astype(F32) + normed(dot(mid_mix, w_mproj[...]))).astype(BF16)
-    wide = dot(spread[...], mid_result).reshape(rows // 2, 2 * TILE, mid_result.shape[1])
+    wide = dot(spread[...].astype(BF16), mid_result).reshape(rows // 2, 2 * TILE, mid_result.shape[1])
     mid_out[...] = wide[:, : cols // 2].astype(BF16)
     fine_copy.wait()
+    for _, copy in copies:
+        copy.wait_send()
 
 
 def statics(rows, cols):
@@ -297,9 +326,9 @@
         jnp.asarray(k_static),
         jnp.asarray(mid[:, None]),
         jnp.asarray(mid[None, :]),
-        jnp.asarray(block, BF16),
-        jnp.asarray(perm, BF16),
-        jnp.asarray(spread, BF16),
+        jnp.asarray(block),
+        jnp.asarray(perm),
+        jnp.asarray(spread),
     )
 
 
@@ -319,40 +348,47 @@
     rows, cols, width = fine_tokens.shape
     blocks = cols // TILE
     tokens = fine_tokens.reshape(rows, blocks, TILE, width)
-    side, latr = exchange(tokens, lat_count, lon_count)
     smem = pl.BlockSpec(memory_space=pltpu.SMEM)
     vmem = pl.BlockSpec(memory_space=pltpu.VMEM)
     anywhere = pl.BlockSpec(memory_space=pl.ANY)
     weights = (fine_qkv, fine_proj, merge_weight, mid_qkv, mid_proj)
+    tables = statics(rows, cols)
     bands = (rows + WLAT) // WLAT
+    reach = WLAT * (cols + 2 * TILE)
     fine_out, mid_out = pl.pallas_call(
-        functools.partial(body_kernel, lat_count),
+        functools.partial(body_kernel, lat_count, lon_count),
         out_shape=(
             jax.ShapeDtypeStruct(tokens.shape, BF16),
             jax.ShapeDtypeStruct((rows // 2, cols // 2, merge_weight.shape[1]), BF16),
         ),
-        in_specs=[smem] * 3 + [vmem] * 7 + [anywhere] * 8,
+        in_specs=[smem] * 3 + [anywhere] * 13,
         out_specs=(anywhere, vmem),
         scratch_shapes=[
             pltpu.VMEM((rows + WLAT,) + tokens.shape[1:], BF16),
-            pltpu.VMEM(side.shape, BF16),
+            pltpu.VMEM((rows + WLAT, 2, TILE, width), BF16),
         ]
+        + [pltpu.VMEM(t.shape, t.dtype) for t in tables]
         + [pltpu.VMEM(w.shape, BF16) for w in weights]
         + [
+            pltpu.VMEM((bands, WLAT * cols, width), BF16),
+            pltpu.VMEM((bands, reach, width), BF16),
+            pltpu.VMEM((bands, reach, width), BF16),
             pltpu.VMEM((bands, WLAT * cols, width), F32),
             pltpu.VMEM(tokens.shape, BF16),
-            pltpu.SemaphoreType.DMA((9,)),
+            pltpu.SemaphoreType.DMA((13,)),
             pltpu.SemaphoreType.DMA,
+            pltpu.SemaphoreType.DMA((8,)),
+            pltpu.SemaphoreType.DMA((8,)),
         ],
-        compiler_params=pltpu.CompilerParams(vmem_limit_bytes=50 * 1024 * 1024),
+        compiler_params=pltpu.CompilerParams(
+            collective_id=0, has_side_effects=True, vmem_limit_bytes=60 * 1024 * 1024
+        ),
     )(
         fine_scale,
         mid_scale,
         window_mask,
-        *statics(rows, cols),
+        *tables,
         tokens,
-        side,
-        latr,
         *weights,
     )
     return fine_out.reshape(rows, cols, width), mid_out

time: 46.7 us -> 33.2 us (0.71)
  local copies, waits for them, and re-layouts: 13.3 us -> 4.06 us
  Pallas kernels: 32.2 us -> 28.2 us
    unnamed x30 -> x2, local copies, waits for them, and re-layouts: 13.3 us -> 4.06 us
    pallas_call x2 -> x1, Pallas kernels: 32.2 us -> 28.2 us  [per_device(): pl.pallas_call(functools.partial(body_kernel, lat_count, lon_count), out_...]
where the time goes in v2:
time: 33.2 us; the launch traced here: 32.9 us
  Pallas kernels  28.2 us (85%)
  local copies, waits for them, and re-layouts  4.06 us (12%)
  between operations  0.64 us (2%)
    pallas_call x1, Pallas kernels, per_device(): pl.pallas_call(functools.partial(body_kernel, lat_count, lon_count), out_...  28.2 us
    unnamed x2, local copies, waits for them, and re-layouts  4.06 us

profile of v2, /device:TPU:0, one launch (start us, length us, event | category | flops | bytes accessed | tf_op | source)
XLA Modules:
  0.0 32.9 jit_solution(1261469633373440936)
XLA Ops:
  0.6 28.2 %shard_map.167 = (bf16[36,3,8,512]{3,2,1,0:T(8,128)(2,1)}, bf16[18,12,1024]{2,1,0:T(8,128)(2,1)}) custom-call(f32[8]{0:T(128)} %fine_scale.1, f32[8]{0:T(128)} %mid_scale.1, s32[13,32]{1,0:T(8,128)} %window_mask.1, s32[144,3]{1,0:T(8,128)} %constant.14.clone.q_static_hbm, s32[3,240]{1,0:T(4,128)} %constant.15.clone.k_static_hbm, ...), custom_call_target="tpu_custom_call" | custom-call | tf_op jit(solution)/shard_map/pallas_call | solution.py:358
  28.8 2.1 %copy.20 = bf16[36,24,512]{2,1,0:T(8,128)(2,1)} copy(bf16[36,24,512]{2,1,0:T(8,128)(2,1)} %bitcast.2) | data formatting | bytes 1769472
  31.0 1.9 %copy.21 = bf16[18,12,1024]{2,1,0:T(8,128)(2,1)} copy(bf16[18,12,1024]{2,1,0:T(8,128)(2,1)} %get-tuple-element.9) | data formatting | bytes 884736

commit v3 on v2

--- a/solution.py
+++ b/solution.py
@@ -116,46 +116,27 @@
     return jnp.concatenate(mixed, axis=1)
 
 
-def body_kernel(
+def attention_kernel(
     lat_count,
     lon_count,
     fine_scale,
-    mid_scale,
     window_mask,
     q_static_hbm,
     k_static_hbm,
-    mid_q_hbm,
-    mid_k_hbm,
     block_hbm,
-    perm_hbm,
-    spread_hbm,
     tokens,
     fine_qkv,
-    fine_proj,
-    merge_weight,
-    mid_qkv,
-    mid_proj,
-    fine_out,
-    mid_out,
+    mix_out,
     core,
     halo,
     q_static,
     k_static,
-    mid_q,
-    mid_k,
     ones_block,
-    perm,
-    spread,
     w_qkv,
-    w_proj,
-    w_merge,
-    w_mqkv,
-    w_mproj,
     q_s,
     k_s,
     v_s,
     mix,
-    out_buf,
     sem,
     out_sem,
     send_sem,
@@ -180,14 +161,6 @@
                 (block_hbm, ones_block),
                 (q_static_hbm, q_static),
                 (k_static_hbm, k_static),
-                (fine_proj, w_proj),
-                (perm_hbm, perm),
-                (merge_weight, w_merge),
-                (mid_qkv, w_mqkv),
-                (mid_q_hbm, mid_q),
-                (mid_k_hbm, mid_k),
-                (mid_proj, w_mproj),
-                (spread_hbm, spread),
             ]
         )
     ]
@@ -198,7 +171,7 @@
         copy.start()
     lat, lon = lax.axis_index("lat"), lax.axis_index("lon")
     fine_row = scale_lanes(fine_scale, width // HEAD)
-    for load in loads[:5]:
+    for load in loads:
         load.wait()
     blocks_of = ones_block[...].astype(BF16)
 
@@ -236,7 +209,8 @@
     k_win, k_lat, k_lon = k_static[0:1], k_static[1:2], k_static[2:3]
     per_row = window_mask.shape[1]
 
-    def band_step(b, carry):
+    written = []
+    for b in range(bands):
         q_code, k_code = q_win * 4, k_win * 4
         for w in range(cols // WLON + 1):
             column = lax.rem(lon * (cols // WLON) + w - 1 + per_row, per_row)
@@ -244,28 +218,87 @@
             by_lat, by_lon = (pattern & 1) * 2, (pattern >> 1) & 1
             q_code = q_code + jnp.where(q_win == w, q_lat * by_lat + q_lon * by_lon, 0)
             k_code = k_code + jnp.where(k_win == w, k_lat * by_lat + k_lon * by_lon, 0)
-        no_north = (lat == 0) & (b == 0)
-        no_south = (lat == lat_count - 1) & (b == bands - 1)
+        no_north = (lat == 0) if b == 0 else False
+        no_south = (lat == lat_count - 1) if b == bands - 1 else False
         gone_low = jnp.where(no_north, 1, 0)
         gone_high = jnp.where(no_south, 1, 0)
         gone = (1 - k_lat) * gone_low + k_lat * gone_high
         k_code = jnp.where((gone > 0) | (k_win < 0), -1, k_code)
         allowed = jnp.where(q_code == k_code, 1.0, 0.0).astype(F32)
-        mix[b] = attend(q_s[b], k_s[b], v_s[b], allowed)
-        return carry
-
-    lax.fori_loop(0, bands, band_step, 0)
-
-    for load in loads[5:]:
+        mix[b] = attend(q_s[b], k_s[b], v_s[b], allowed).astype(BF16)
+        write = pltpu.make_async_copy(mix.at[b], mix_out.at[b], out_sem.at[b])
+        write.start()
+        written.append(write)
+    for write in written:
+        write.wait()
+    for _, copy in copies:
+        copy.wait_send()
+
+
+def tail_kernel(
+    mid_scale,
+    mix_hbm,
+    tokens,
+    fine_proj,
+    perm_hbm,
+    merge_weight,
+    mid_qkv,
+    block_hbm,
+    mid_q_hbm,
+    mid_k_hbm,
+    mid_proj,
+    spread_hbm,
+    fine_out,
+    mid_out,
+    mix,
+    core,
+    w_proj,
+    perm,
+    w_merge,
+    w_mqkv,
+    ones_block,
+    mid_q,
+    mid_k,
+    w_mproj,
+    spread,
+    out_buf,
+    sem,
+    out_sem,
+):
+    rows, blocks, _, width = tokens.shape
+    half = WLAT // 2
+    cols = blocks * TILE
+    bands = (rows + WLAT) // WLAT
+    loads = [
+        pltpu.make_async_copy(src, dst, sem.at[n])
+        for n, (src, dst) in enumerate(
+            [
+                (mix_hbm, mix),
+                (tokens, core),
+                (fine_proj, w_proj),
+                (perm_hbm, perm),
+                (merge_weight, w_merge),
+                (mid_qkv, w_mqkv),
+                (block_hbm, ones_block),
+                (mid_q_hbm, mid_q),
+                (mid_k_hbm, mid_k),
+                (mid_proj, w_mproj),
+                (spread_hbm, spread),
+            ]
+        )
+    ]
+    for load in loads:
+        load.start()
+    for load in loads[:4]:
         load.wait()
     mover = perm[...].astype(BF16)
     chunk = 2 * WLAT
     size = chunk * cols
     merged_in = []
-    flat = mix[...].reshape(bands * WLAT * cols, width)
+    flat = mix[...].astype(F32).reshape(bands * WLAT * cols, width)
     for c in range(rows // chunk):
         start = half * cols + c * size
-        x = core[pl.ds(half + c * chunk, chunk)].astype(F32).reshape(size, width)
+        x = core[pl.ds(c * chunk, chunk)].astype(F32).reshape(size, width)
         projected = dot(flat[start : start + size].astype(BF16), w_proj[...])
         result = x + normed(projected)
         out_buf[pl.ds(c * chunk, chunk)] = result.reshape(chunk, blocks, TILE, width).astype(BF16)
@@ -277,6 +310,9 @@
         merged_in.append(normed(quads))
     fine_copy = pltpu.make_async_copy(out_buf, fine_out, out_sem)
     fine_copy.start()
+    for load in loads[4:]:
+        load.wait()
+    blocks_of = ones_block[...].astype(BF16)
     merge_in = jnp.concatenate(merged_in, axis=0).astype(BF16)
     merged = dot(merge_in, w_merge[...]).astype(BF16)
     mid_width = mid_proj.shape[0]
@@ -291,8 +327,6 @@
     wide = dot(spread[...].astype(BF16), mid_result).reshape(rows // 2, 2 * TILE, mid_result.shape[1])
     mid_out[...] = wide[:, : cols // 2].astype(BF16)
     fine_copy.wait()
-    for _, copy in copies:
-        copy.wait_send()
 
 
 def statics(rows, cols):
@@ -351,46 +385,65 @@
     smem = pl.BlockSpec(memory_space=pltpu.SMEM)
     vmem = pl.BlockSpec(memory_space=pltpu.VMEM)
     anywhere = pl.BlockSpec(memory_space=pl.ANY)
-    weights = (fine_qkv, fine_proj, merge_weight, mid_qkv, mid_proj)
-    tables = statics(rows, cols)
+    q_static, k_static, mid_q, mid_k, block, perm, spread = statics(rows, cols)
     bands = (rows + WLAT) // WLAT
     reach = WLAT * (cols + 2 * TILE)
-    fine_out, mid_out = pl.pallas_call(
-        functools.partial(body_kernel, lat_count, lon_count),
-        out_shape=(
-            jax.ShapeDtypeStruct(tokens.shape, BF16),
-            jax.ShapeDtypeStruct((rows // 2, cols // 2, merge_weight.shape[1]), BF16),
-        ),
-        in_specs=[smem] * 3 + [anywhere] * 13,
-        out_specs=(anywhere, vmem),
+    held = pltpu.CompilerParams(vmem_limit_bytes=60 * 1024 * 1024)
+    first = (q_static, k_static, block, tokens, fine_qkv)
+    mix = pl.pallas_call(
+        functools.partial(attention_kernel, lat_count, lon_count),
+        out_shape=jax.ShapeDtypeStruct((bands, WLAT * cols, width), BF16),
+        in_specs=[smem] * 2 + [anywhere] * len(first),
+        out_specs=anywhere,
         scratch_shapes=[
             pltpu.VMEM((rows + WLAT,) + tokens.shape[1:], BF16),
             pltpu.VMEM((rows + WLAT, 2, TILE, width), BF16),
-        ]
-        + [pltpu.VMEM(t.shape, t.dtype) for t in tables]
-        + [pltpu.VMEM(w.shape, BF16) for w in weights]
-        + [
+            pltpu.VMEM(q_static.shape, q_static.dtype),
+            pltpu.VMEM(k_static.shape, k_static.dtype),
+            pltpu.VMEM(block.shape, block.dtype),
+            pltpu.VMEM(fine_qkv.shape, BF16),
             pltpu.VMEM((bands, WLAT * cols, width), BF16),
             pltpu.VMEM((bands, reach, width), BF16),
             pltpu.VMEM((bands, reach, width), BF16),
-            pltpu.VMEM((bands, WLAT * cols, width), F32),
-            pltpu.VMEM(tokens.shape, BF16),
-            pltpu.SemaphoreType.DMA((13,)),
-            pltpu.SemaphoreType.DMA,
+            pltpu.VMEM((bands, WLAT * cols, width), BF16),
+            pltpu.SemaphoreType.DMA((len(first),)),
+            pltpu.SemaphoreType.DMA((bands,)),
             pltpu.SemaphoreType.DMA((8,)),
             pltpu.SemaphoreType.DMA((8,)),
         ],
         compiler_params=pltpu.CompilerParams(
             collective_id=0, has_side_effects=True, vmem_limit_bytes=60 * 1024 * 1024
         ),
-    )(
-        fine_scale,
-        mid_scale,
-        window_mask,
-        *tables,
+    )(fine_scale, window_mask, *first)
+    second = (
+        mix,
         tokens,
-        *weights,
-    )
+        fine_proj,
+        perm,
+        merge_weight,
+        mid_qkv,
+        block,
+        mid_q,
+        mid_k,
+        mid_proj,
+        spread,
+    )
+    fine_out, mid_out = pl.pallas_call(
+        tail_kernel,
+        out_shape=(
+            jax.ShapeDtypeStruct(tokens.shape, BF16),
+            jax.ShapeDtypeStruct((rows // 2, cols // 2, merge_weight.shape[1]), BF16),
+        ),
+        in_specs=[smem] + [anywhere] * len(second),
+        out_specs=(anywhere, vmem),
+        scratch_shapes=[pltpu.VMEM(a.shape, a.dtype) for a in second]
+        + [
+            pltpu.VMEM(tokens.shape, BF16),
+            pltpu.SemaphoreType.DMA((len(second),)),
+            pltpu.SemaphoreType.DMA,
+        ],
+        compiler_params=held,
+    )(mid_scale, *second)
     return fine_out.reshape(rows, cols, width), mid_out
 
 

time: 33.2 us -> 29.3 us (0.88)
  local copies, waits for them, and re-layouts: 4.06 us -> 0 us
    unnamed x2 -> x0, local copies, waits for them, and re-layouts: 4.06 us -> none
    pallas_call x1 -> x2, Pallas kernels: 28.2 us -> 28.5 us  [the longest x1 19.1 us: per_device(): pl.pallas_call(functools.partial(attention_kernel, lat_count, lon_count),...]
where the time goes in v3:
time: 29.3 us; the launch traced here: 29.1 us
  Pallas kernels  28.5 us (97%)
  between operations  0.64 us (2%)
    pallas_call x1, Pallas kernels, per_device(): pl.pallas_call(functools.partial(attention_kernel, lat_count, lon_count),...  19.1 us
    pallas_call x1, Pallas kernels, per_device(): pl.pallas_call(tail_kernel, out_shape=(jax.ShapeDtypeStruct(tokens.shape,...  9.38 us

profile of v3, /device:TPU:0, one launch (start us, length us, event | category | flops | bytes accessed | tf_op | source)
XLA Modules:
  0.0 29.1 jit_solution(6127662205833555354)
XLA Ops:
  0.6 19.1 %shard_map.167.mix_hbm = bf16[7,144,512]{2,1,0:T(8,128)(2,1)} custom-call(f32[8]{0:T(128)} %fine_scale.1, s32[13,32]{1,0:T(8,128)} %window_mask.1, s32[144,3]{1,0:T(8,128)} %constant.14.clone.q_static_hbm, s32[3,240]{1,0:T(4,128)} %constant.15.clone.k_static_hbm, f32[256,256]{1,0:T(8,128)} %constant.18.clone.block_hbm, bf16[36,3,8,512]{3,2,1,0:T(8,128)(2,1)} %bitcast.2, ...), custom_call_target="tpu_custom_call" | custom-call | tf_op jit(solution)/shard_map/pallas_call | solution.py:393
  19.7 9.4 %shard_map.168 = (bf16[36,3,8,512]{3,2,1,0:T(8,128)(2,1)}, bf16[18,12,1024]{2,1,0:T(8,128)(2,1)}) custom-call(f32[8]{0:T(128)} %mid_scale.1, bf16[7,144,512]{2,1,0:T(8,128)(2,1)} %shard_map.167.mix_hbm, bf16[36,3,8,512]{3,2,1,0:T(8,128)(2,1)} %bitcast.3, bf16[512,512]{1,0:T(8,128)(2,1)} %fine_proj.1, f32[288,288]{1,0:T(8,128)} %constant.19.clone.perm_hbm, ...), custom_call_target="tpu_custom_call" | custom-call | tf_op jit(solution)/shard_map/pallas_call | solution.py:431
